TPU v7x, 32 devices: a whole 2x2x4 slice. The times are simulated.
32 devices in a mesh: dp: 4 (over y, x), expert: 4 (over z), wshard: 2 (over core).
Axes of the slice: x: 2, y: 2, z: 4, core: 2. Of those that a mesh axis runs over, the one named last changes fastest.
Arguments:
- tokens: bfloat16 [16384, 768], P(('dp', 'expert', 'wshard')), may hold values from -6 to 6
- cotangent: bfloat16 [16384, 768], P(('dp', 'expert', 'wshard')), may hold values from -6 to 6
- segment_ids: int32 [32, 512], P(('dp', 'expert', 'wshard')), may hold values from 0 to 3, never falling along the last dimension, each value on 1 to 256 neighbouring positions
- routes: int32 [16384, 2], P(('dp', 'expert', 'wshard')), may hold values from 0 to 7, all different within a row; in each aligned block of 512 rows (0 to 511, 512 to 1023, ...) at most 160 rows name the same one
- gain_attn: bfloat16 [768], P('wshard'), may hold values from 0.099609375 to 1.8984375
- gain_ffn: bfloat16 [768], P('wshard'), may hold values from 0.099609375 to 1.8984375
- w_query: bfloat16 [768, 768], P('wshard'), may hold values from -0.21875 to 0.21875
- w_key: bfloat16 [768, 768], P('wshard'), may hold values from -0.21875 to 0.21875
- w_value: bfloat16 [768, 768], P('wshard'), may hold values from -0.21875 to 0.21875
- w_project: bfloat16 [768, 768], P('wshard'), may hold values from -0.875 to 0.875
- router: bfloat16 [768, 8], P('wshard'), may hold values from -0.15625 to 0.15625
- bias_table: bfloat16 [12, 32], P('wshard'), may hold values from -4 to 4
- expert_in: bfloat16 [8, 768, 3072], P(('expert', 'wshard')), may hold values from -0.21875 to 0.21875
- expert_out: bfloat16 [8, 3072, 768], P(('expert', 'wshard')), may hold values from -0.21875 to 0.21875
Outputs:
- mixed: bfloat16 [16384, 768], P(('dp', 'expert', 'wshard'))
- grad_tokens: float32 [16384, 768], P(('dp', 'expert', 'wshard'))
- grad_gain_attn: float32 [768], P('wshard')
- grad_gain_ffn: float32 [768], P('wshard')
- grad_w_query: float32 [768, 768], P('wshard')
- grad_w_key: float32 [768, 768], P('wshard')
- grad_w_value: float32 [768, 768], P('wshard')
- grad_w_project: float32 [768, 768], P('wshard')
- grad_router: float32 [768, 8], P('wshard')
- grad_bias_table: float32 [12, 32], P('wshard')
- grad_expert_in: float32 [8, 768, 3072], P(('expert', 'wshard'), None, 'dp')
- grad_expert_out: float32 [8, 3072, 768], P(('expert', 'wshard'), 'dp')
Inputs may be any that keep to these rules, and one draw needn't show every extreme that they name: `routes`: in the rows of one device no expert is named more than 160 times, a bound that some block reaches; the two experts of a token differ. `segment_ids`: ids never fall along a sequence.
All inputs are finite; a program needn't handle non-finite values.
Results may differ from a plain program's by a relative error of at most 0.017.
Values may be sent and summed in bfloat16 or wider, within the bound.
A program may use at most 192 MiB of HBM per device.

v0:
```python
import jax
import jax.numpy as jnp
import numpy as np
from jax import lax
from jax.sharding import PartitionSpec as P

BUCKETS = 32
MAX_DISTANCE = 128


EPS = 1e-06


def bucket_edges():
    half = BUCKETS // 2
    spans = np.arange(half, MAX_DISTANCE)
    levels = half + np.floor(
        np.log(spans / float(half)) / np.log(MAX_DISTANCE / float(half)) * half
    ).astype(np.int64)
    return [
        int(spans[levels >= level][0])
        for level in range(half + 1, BUCKETS)
        if np.any(levels >= level)
    ]


def bucket_of(distance):
    distance = jnp.maximum(distance, 0)
    bucket = jnp.minimum(distance, BUCKETS // 2)
    for edge in bucket_edges():
        bucket = bucket + (distance >= edge).astype(jnp.int32)
    return bucket


def contract(left, right, left_dim, right_dim):
    return lax.dot_general(
        left, right, (((left_dim,), (right_dim,)), ((), ())), preferred_element_type=jnp.float32
    )


def send_rows(rows):
    moved = lax.all_to_all(rows, ("expert", "wshard"), split_axis=0, concat_axis=0, tiled=True)
    return moved


def send_results(rows):
    moved = lax.all_to_all(rows, ("expert", "wshard"), split_axis=0, concat_axis=0, tiled=True)
    return moved


def send_grads(rows):
    moved = lax.all_to_all(rows, ("expert", "wshard"), split_axis=0, concat_axis=0, tiled=True)
    return moved


def send_row_grads(rows):
    moved = lax.all_to_all(rows, ("expert", "wshard"), split_axis=0, concat_axis=0, tiled=True)
    return moved


def block_scores(query_block, key_rows, start, segment, table, block, length, scale):
    rows = start + jnp.arange(block, dtype=jnp.int32)
    distance = rows[:, None] - jnp.arange(length, dtype=jnp.int32)[None, :]
    allowed = (distance >= 0) & (segment[:, None] == segment[None, :])
    onehot = (bucket_of(distance)[..., None] == jnp.arange(BUCKETS, dtype=jnp.int32)).astype(
        jnp.bfloat16
    )
    bias = jnp.einsum("qkb,hb->hqk", onehot, table, preferred_element_type=jnp.float32)
    raw = jnp.einsum("qhd,khd->hqk", query_block, key_rows, preferred_element_type=jnp.float32)
    scores = raw * scale + bias
    return (jnp.where(allowed[None], scores, -1e30), onehot)


def norm_back(grad_normed, inputs, rms, gain):
    unit = inputs * rms
    grad_gain = jnp.sum(grad_normed * unit, axis=0)
    scaled = grad_normed * gain
    return (grad_gain, rms * (scaled - unit * jnp.mean(scaled * unit, axis=-1, keepdims=True)))


def per_device(
    tokens,
    cotangent,
    segment_ids,
    routes,
    gain_attn,
    gain_ffn,
    w_query,
    w_key,
    w_value,
    w_project,
    router,
    bias_table,
    expert_in,
    expert_out,
):
    gathered = (
        lax.all_gather(gain_attn, "wshard", axis=0, tiled=True),
        lax.all_gather(gain_ffn, "wshard", axis=0, tiled=True),
        lax.all_gather(w_query, "wshard", axis=0, tiled=True),
        lax.all_gather(w_key, "wshard", axis=0, tiled=True),
        lax.all_gather(w_value, "wshard", axis=0, tiled=True),
        lax.all_gather(w_project, "wshard", axis=0, tiled=True),
        lax.all_gather(router, "wshard", axis=0, tiled=True),
        lax.all_gather(bias_table, "wshard", axis=0, tiled=True),
    )
    gain_one, gain_two, query_full, key_full, value_full, project_full, router_full, table_full = (
        gathered
    )
    gain_one = gain_one.astype(jnp.float32)
    gain_two = gain_two.astype(jnp.float32)
    length, width = tokens.shape
    heads = table_full.shape[0]
    head_size = width // heads
    experts = router_full.shape[1]
    capacity = 5 * length // (2 * experts)
    block = min(512, length)
    scale = head_size ** (-0.5)
    segment = segment_ids[0]
    starts = jnp.arange(length // block, dtype=jnp.int32) * block
    flat = routes.reshape(-1)
    onehot_int = (flat[:, None] == jnp.arange(experts, dtype=jnp.int32)[None, :]).astype(jnp.int32)
    slot_place = jnp.sum(jnp.cumsum(onehot_int, axis=0) * onehot_int, axis=-1) - 1
    dest = (flat * capacity + slot_place).reshape(length, 2)
    slots = jnp.arange(experts * capacity, dtype=jnp.int32)
    takes_first = slots[:, None] == dest[None, :, 0]
    takes_second = slots[:, None] == dest[None, :, 1]
    spread = (takes_first | takes_second).astype(jnp.bfloat16)
    pick_first = (dest[:, 0][:, None] == slots[None, :]).astype(jnp.bfloat16)
    pick_second = (dest[:, 1][:, None] == slots[None, :]).astype(jnp.bfloat16)

    def to_slots(rows):
        placed = jnp.dot(spread, rows, preferred_element_type=jnp.float32).astype(jnp.bfloat16)
        return placed.reshape(experts, capacity, width)

    cotangent_arrived = send_grads(to_slots(cotangent)).reshape(-1, width)
    inputs = tokens.astype(jnp.float32)
    rms_one = lax.rsqrt(jnp.mean(inputs * inputs, axis=-1, keepdims=True) + EPS)
    normed = (inputs * rms_one * gain_one).astype(jnp.bfloat16)
    joined_weight = jnp.concatenate([query_full, key_full, value_full], axis=1)
    projected = jnp.dot(normed, joined_weight, preferred_element_type=jnp.float32).astype(
        jnp.bfloat16
    )
    queries = projected[:, :width].reshape(length, heads, head_size)
    key_rows = projected[:, width : 2 * width].reshape(length, heads, head_size)
    value_rows = projected[:, 2 * width :].reshape(length, heads, head_size)

    def forward_block(start):
        masked, onehot = block_scores(
            queries, key_rows, start, segment, table_full, block, length, scale
        )
        highest = jnp.max(masked, axis=-1, keepdims=True)
        expo = jnp.exp(masked - highest)
        total = jnp.sum(expo, axis=-1, keepdims=True)
        probs = expo / total
        logsum = highest[..., 0] + jnp.log(total[..., 0])
        result = jnp.einsum(
            "hqk,khd->qhd",
            probs.astype(jnp.bfloat16),
            value_rows,
            preferred_element_type=jnp.float32,
        )
        return (result, logsum)

    attended, logsums = lax.map(forward_block, starts)
    attended = attended.reshape(length, width).astype(jnp.bfloat16)
    branch = jnp.dot(attended, project_full, preferred_element_type=jnp.float32)
    resid = inputs + branch
    rms_two = lax.rsqrt(jnp.mean(resid * resid, axis=-1, keepdims=True) + EPS)
    normed_two = (resid * rms_two * gain_two).astype(jnp.bfloat16)
    logits = jnp.dot(normed_two, router_full, preferred_element_type=jnp.float32)
    chosen_mask = routes[..., None] == jnp.arange(experts, dtype=jnp.int32)
    chosen = jnp.sum(jnp.where(chosen_mask, logits[:, None, :], 0.0), axis=-1)
    gates = jax.nn.softmax(chosen, axis=-1)
    normed_two, cotangent_arrived = lax.optimization_barrier((normed_two, cotangent_arrived))
    arrived = send_rows(to_slots(normed_two))
    gate_slots = jnp.sum(
        jnp.where(takes_first, gates[:, 0][None, :], 0.0)
        + jnp.where(takes_second, gates[:, 1][None, :], 0.0),
        axis=1,
    )
    gate_arrived = send_rows(gate_slots.reshape(experts, capacity)).reshape(-1)
    arrived, gate_arrived = lax.optimization_barrier((arrived, gate_arrived))
    rows_in = arrived.reshape(-1, width)
    pre = jnp.dot(rows_in, expert_in[0], preferred_element_type=jnp.float32)
    hidden = jax.nn.gelu(pre).astype(jnp.bfloat16)
    produced = jnp.dot(hidden, expert_out[0], preferred_element_type=jnp.float32).astype(
        jnp.bfloat16
    )
    produced, gate_arrived = lax.optimization_barrier((produced, gate_arrived))
    returned = send_results(produced.reshape(experts, capacity, width)).reshape(-1, width)
    grad_arrived = (gate_arrived[:, None] * cotangent_arrived.astype(jnp.float32)).astype(
        jnp.bfloat16
    )
    grad_out_weight = contract(hidden, grad_arrived, 0, 0).astype(jnp.bfloat16)
    grad_hidden = contract(grad_arrived, expert_out[0], 1, 1)
    unused, gelu_back = jax.vjp(jax.nn.gelu, pre)
    grad_pre = gelu_back(grad_hidden)[0].astype(jnp.bfloat16)
    grad_in_weight = contract(rows_in, grad_pre, 0, 0).astype(jnp.bfloat16)
    grad_pre, grad_in_weight, grad_out_weight = lax.optimization_barrier(
        (grad_pre, grad_in_weight, grad_out_weight)
    )
    expert_out_sum = lax.psum_scatter(
        grad_out_weight[None], "dp", scatter_dimension=1, tiled=True
    )
    expert_in_sum = lax.psum_scatter(grad_in_weight[None], "dp", scatter_dimension=2, tiled=True)
    grad_rows = contract(grad_pre, expert_in[0], 1, 1).astype(jnp.bfloat16)
    returned, grad_rows = lax.optimization_barrier((returned, grad_rows))
    grad_back = send_row_grads(grad_rows.reshape(experts, capacity, width)).reshape(-1, width)
    picked_first = jnp.dot(pick_first, returned, preferred_element_type=jnp.float32)
    picked_second = jnp.dot(pick_second, returned, preferred_element_type=jnp.float32)
    mixed = resid + (gates[:, :1] * picked_first + gates[:, 1:] * picked_second)
    grad_out = cotangent.astype(jnp.float32)
    grad_gates = jnp.stack(
        [jnp.sum(grad_out * picked_first, axis=-1), jnp.sum(grad_out * picked_second, axis=-1)],
        axis=-1,
    )
    grad_normed_two = jnp.dot(
        pick_first + pick_second, grad_back, preferred_element_type=jnp.float32
    )
    grad_chosen = gates * (grad_gates - jnp.sum(gates * grad_gates, axis=-1, keepdims=True))
    grad_logits = jnp.sum(jnp.where(chosen_mask, grad_chosen[..., None], 0.0), axis=1).astype(
        jnp.bfloat16
    )
    grad_router = contract(normed_two, grad_logits, 0, 0)
    grad_normed_two = grad_normed_two + contract(grad_logits, router_full, 1, 1)
    grad_gain_two, grad_resid_norm = norm_back(grad_normed_two, resid, rms_two, gain_two)
    grad_resid = grad_out + grad_resid_norm
    grad_branch = grad_resid.astype(jnp.bfloat16)
    grad_project = contract(attended, grad_branch, 0, 0)
    grad_attended = (
        contract(grad_branch, project_full, 1, 1)
        .astype(jnp.bfloat16)
        .reshape(length, heads, head_size)
    )

    def backward_block(carry, inputs_block):
        grad_keys, grad_values, grad_table = carry
        start, logsum = inputs_block
        masked, onehot = block_scores(
            queries, key_rows, start, segment, table_full, block, length, scale
        )
        probs = jnp.exp(masked - logsum[..., None])
        grad_probs = jnp.einsum(
            "qhd,khd->hqk", grad_attended, value_rows, preferred_element_type=jnp.float32
        )
        inner = jnp.sum(probs * grad_probs, axis=-1, keepdims=True)
        grad_scores = (probs * (grad_probs - inner)).astype(jnp.bfloat16)
        grad_query_block = (
            jnp.einsum("hqk,khd->qhd", grad_scores, key_rows, preferred_element_type=jnp.float32)
            * scale
        )
        grad_keys = (
            grad_keys
            + jnp.einsum("hqk,qhd->khd", grad_scores, queries, preferred_element_type=jnp.float32)
            * scale
        )
        grad_values = grad_values + jnp.einsum(
            "hqk,qhd->khd",
            probs.astype(jnp.bfloat16),
            grad_attended,
            preferred_element_type=jnp.float32,
        )
        grad_table = grad_table + jnp.einsum(
            "hqk,qkb->hb", grad_scores, onehot, preferred_element_type=jnp.float32
        )
        return ((grad_keys, grad_values, grad_table), grad_query_block)

    zero_rows = jnp.zeros((length, heads, head_size), jnp.float32)
    start_carry = (zero_rows, zero_rows, jnp.zeros((heads, BUCKETS), jnp.float32))
    (grad_keys, grad_values, grad_table), grad_queries = lax.scan(
        backward_block, start_carry, (starts, logsums)
    )
    grad_joined = jnp.concatenate(
        [
            grad_queries.reshape(length, width),
            grad_keys.reshape(length, width),
            grad_values.reshape(length, width),
        ],
        axis=1,
    ).astype(jnp.bfloat16)
    grad_weights = contract(normed, grad_joined, 0, 0)
    grad_normed = contract(grad_joined, joined_weight, 1, 1)
    grad_gain_one, grad_input_norm = norm_back(grad_normed, inputs, rms_one, gain_one)
    grad_tokens = grad_resid + grad_input_norm
    half = width // 2
    group = lax.axis_size("dp") * lax.axis_size("expert") * 8
    small = jnp.concatenate(
        [
            grad_gain_one.reshape(2, -1),
            grad_gain_two.reshape(2, -1),
            grad_router.reshape(2, -1),
            grad_table.reshape(2, -1),
        ],
        axis=1,
    ).astype(jnp.bfloat16)
    edges = np.cumsum([0, half, half, half * experts, heads // 2 * BUCKETS])
    extra = -(-int(edges[-1]) // (group * width)) * group
    small = jnp.pad(small, ((0, 0), (0, extra * width - int(edges[-1])))).reshape(2, extra, width)
    large = jnp.stack(
        [
            grad_weights[:, :width],
            grad_weights[:, width : 2 * width],
            grad_weights[:, 2 * width :],
            grad_project,
        ]
    ).astype(jnp.bfloat16)
    large = large.reshape(4, 2, half, width).transpose(1, 0, 2, 3).reshape(2, 4 * half, width)
    large = jnp.concatenate([large, small], axis=1)
    core = lax.axis_index("wshard")
    keep = lax.dynamic_index_in_dim(large, core, 0, keepdims=False)
    give = lax.dynamic_index_in_dim(large, 1 - core, 0, keepdims=False)
    got = lax.ppermute(give, "wshard", [(0, 1), (1, 0)])
    part = (keep.astype(jnp.float32) + got.astype(jnp.float32)).astype(jnp.bfloat16)
    for axis in ("dp", "expert"):
        pieces = lax.all_to_all(
            part.reshape(lax.axis_size(axis), -1, width), axis, split_axis=0, concat_axis=0, tiled=True
        )
        part = jnp.sum(pieces.astype(jnp.float32), axis=0).astype(jnp.bfloat16)
    for axis in ("expert", "dp"):
        part = lax.all_gather(part, axis, axis=0, tiled=True)
    small = part[4 * half :].reshape(-1).astype(jnp.float32)
    part = part[: 4 * half].reshape(4, half, width).astype(jnp.float32)

    def own(index, shape):
        return small[edges[index] : edges[index + 1]].reshape(shape)

    shares = (
        own(0, (half,)),
        own(1, (half,)),
        part[0],
        part[1],
        part[2],
        part[3],
        own(2, (half, experts)),
        own(3, (heads // 2, BUCKETS)),
    )
    expert_in_grad = expert_in_sum.astype(jnp.float32)
    expert_out_grad = expert_out_sum.astype(jnp.float32)
    return (
        mixed.astype(jnp.bfloat16),
        grad_tokens,
        shares[0],
        shares[1],
        shares[2],
        shares[3],
        shares[4],
        shares[5],
        shares[6],
        shares[7],
        expert_in_grad,
        expert_out_grad,
    )


def solution(mesh):
    return jax.shard_map(
        per_device,
        mesh=mesh,
        in_specs=(
            P(("dp", "expert", "wshard"), None),
            P(("dp", "expert", "wshard"), None),
            P(("dp", "expert", "wshard"), None),
            P(("dp", "expert", "wshard"), None),
            P("wshard"),
            P("wshard"),
            P("wshard", None),
            P("wshard", None),
            P("wshard", None),
            P("wshard", None),
            P("wshard", None),
            P("wshard", None),
            P(("expert", "wshard"), None, None),
            P(("expert", "wshard"), None, None),
        ),
        out_specs=(
            P(("dp", "expert", "wshard"), None),
            P(("dp", "expert", "wshard"), None),
            P("wshard"),
            P("wshard"),
            P("wshard", None),
            P("wshard", None),
            P("wshard", None),
            P("wshard", None),
            P("wshard", None),
            P("wshard", None),
            P(("expert", "wshard"), None, "dp"),
            P(("expert", "wshard"), "dp", None),
        ),
        check_vma=False,
    )
```

profile of v0, /device:TPU:0, one launch (start us, length us, event | category | flops | bytes accessed | tf_op | source)
XLA Modules:
  0.0 511.9 jit_solution(17502325581624337251)
XLA Ops:
  9.4 0.8 copy.126
  10.4 2.3 reduce-window.6
  13.8 2.6 convolution_convert_fusion.5
  16.4 6.5 %all-to-all-start = ((bf16[8,160,768]{2,1,0:T(8,128)(2,1)}), bf16[8,160,768]{2,1,0:T(8,128)(2,1)}, u32[]{:S(2)}, u32[]{:S(2)}) async-start(bf16[8,160,768]{2,1,0:T(8,128)(2,1)} %bitcast.154), calls=%async_computation | async-start | bytes 3932160 | tf_op jit(solution)/shard_map/all_to_all | solution.py:52
  24.1 2.0 all-gather
  26.2 1.8 all-gather.2
  28.2 1.8 all-gather.1
  30.1 2.0 all_gather.37
  32.3 8.5 %fusion.1 = f32[512,512,12]{0,2,1:T(8,128)} fusion(bf16[12,32,1]{1,0,2:T(8,128)(2,1)S(1)} %reshape.432, s32[512,512]{0,1:T(8,128)S(1)} %convert_add_fusion.3), kind=kOutput, calls=%fused_computation.2 | convolution fusion | flops 209715200 | bytes 13632256 | tf_op jit(solution)/shard_map/while/body/eval_jaxpr/qkb,hb->hqk/dot_general | solution.py:68
  40.7 2.5 constant_dynamic-update-slice_fusion.2
  43.3 2.5 constant_dynamic-update-slice_fusion.1
  45.7 2.4 constant_dynamic-update-slice_fusion
  48.1 4.1 convolution_convert_fusion.3
  53.3 16.0 %fusion.127 = (f32[12,512]{1,0:T(8,128)S(1)}, f32[12,512,512]{1,2,0:T(8,128)S(1)}) fusion(f32[512,512,12]{0,2,1:T(8,128)} %fusion.1, bf16[512,12,64]{0,2,1:T(8,128)(2,1)S(1)} %bitcast.140, bf16[512,12,64]{0,2,1:T(8,128)(2,1)S(1)} %bitcast.135, pred[512,512]{0,1:T(8,128)(4,1)S(1)} %fusion.97), kind=kOutput, calls=%fused_computation.188 | convolution fusion | flops 415229952 | bytes 27025408 | tf_op jit(solution)/shard_map/while/body/eval_jaxpr/qhd,khd->hqk/dot_general | solution.py:69
  69.3 1.8 fusion.12
  71.2 2.8 copy-done
  74.0 3.2 fusion.61
  77.2 2.4 multiply_reduce_fusion.3
  81.6 4.9 all-to-all-start.2
  86.5 2.6 convolution_convert_fusion.4
  89.1 3.0 all-to-all-done.2
  92.1 4.4 all-to-all-start.1
  96.6 46.1 %all-to-all-done.1 = bf16[8,160,768]{2,1,0:T(8,128)(2,1)} async-done(((bf16[8,160,768]{2,1,0:T(8,128)(2,1)}), bf16[8,160,768]{2,1,0:T(8,128)(2,1)}, u32[]{:S(2)}, u32[]{:S(2)}) %all-to-all-start.1) | async-done | bytes 1966112 | tf_op jit(solution)/shard_map/all_to_all | solution.py:42
  142.7 8.7 %fusion.25 = f32[1280,3072]{1,0:T(8,128)S(1)} fusion(bf16[1280,768]{1,0:T(8,128)(2,1)} %bitcast.16, bf16[1,768,3072]{2,1,0:T(8,128)(2,1)} %param.26), kind=kOutput, calls=%fused_computation.41 | convolution fusion | flops 6039797760 | bytes 22413312 | tf_op jit(solution)/shard_map/dot_general | solution.py:185
  151.5 5.5 %copy-done.34 = f32[1280,3072]{1,0:T(8,128)} copy-done((f32[1280,3072]{1,0:T(8,128)}, f32[1280,3072]{1,0:T(8,128)S(1)}, u32[]{:S(2)}) %copy-start.34) | copy-done | bytes 15728664
  157.0 12.7 %fusion.30 = bf16[1280,768]{1,0:T(8,128)(2,1)} fusion(bf16[1,3072,768]{2,1,0:T(8,128)(2,1)} %param.27, f32[1280,3072]{1,0:T(8,128)S(1)} %fusion.25), kind=kOutput, calls=%fused_computation.48 | convolution fusion | flops 6076170240 | bytes 22413312 | tf_op jit(solution)/shard_map/dot_general | solution.py:187
  169.6 14.4 %convolution_convert_fusion = bf16[3072,768]{1,0:T(8,128)(2,1)} fusion(bf16[1280,768]{1,0:T(8,128)(2,1)} %bitcast.13, f32[1280]{0:T(1024)S(1)} %reshape.402, f32[1280,3072]{1,0:T(8,128)} %copy-done.34), kind=kOutput, calls=%fused_computation.32 | convolution fusion | flops 6080495616 | bytes 22418432 | tf_op jit(solution)/shard_map/dot_general | solution.py:36
  184.1 20.0 %fusion.10 = bf16[1280,3072]{1,0:T(8,128)(2,1)} fusion(f32[1280,3072]{1,0:T(8,128)} %copy-done.34, bf16[1,3072,768]{2,1,0:T(8,128)(2,1)S(1)} %bitcast.187, bf16[1280,768]{1,0:T(8,128)(2,1)} %bitcast.13, f32[1280]{0:T(1024)S(1)} %reshape.402), kind=kOutput, calls=%fused_computation.13 | convolution fusion | flops 6121390080 | bytes 30282752 | tf_op jit(solution)/shard_map/dot_general | solution.py:36
  204.1 10.7 %convolution_convert_fusion.2 = bf16[768,3072]{1,0:T(8,128)(2,1)} fusion(bf16[1280,768]{1,0:T(8,128)(2,1)} %bitcast.16, bf16[1280,3072]{1,0:T(8,128)(2,1)} %fusion.10), kind=kOutput, calls=%fused_computation.34 | convolution fusion | flops 6042157056 | bytes 14548992 | tf_op jit(solution)/shard_map/dot_general | solution.py:36
  214.8 4.4 all-to-all-start.3
  219.2 11.8 %fusion.27 = bf16[1280,768]{1,0:T(8,128)(2,1)} fusion(bf16[1280,3072]{1,0:T(8,128)(2,1)} %fusion.10, bf16[1,768,3072]{2,1,0:T(8,128)(2,1)} %param.26), kind=kOutput, calls=%fused_computation.47 | convolution fusion | flops 6040780800 | bytes 14548992 | tf_op jit(solution)/shard_map/dot_general | solution.py:36
  230.9 34.5 %all-to-all-done.3 = bf16[8,160,768]{2,1,0:T(8,128)(2,1)} async-done(((bf16[8,160,768]{2,1,0:T(8,128)(2,1)}), bf16[8,160,768]{2,1,0:T(8,128)(2,1)}, u32[]{:S(2)}, u32[]{:S(2)}) %all-to-all-start.3) | async-done | bytes 1966112 | tf_op jit(solution)/shard_map/all_to_all | solution.py:47
  265.4 4.4 all-to-all-start.4
  270.7 2.8 fusion.34
  273.5 4.0 fusion.55
  278.2 37.9 %all-to-all-done.4 = bf16[8,160,768]{2,1,0:T(8,128)(2,1)} async-done(((bf16[8,160,768]{2,1,0:T(8,128)(2,1)}), bf16[8,160,768]{2,1,0:T(8,128)(2,1)}, u32[]{:S(2)}, u32[]{:S(2)}) %all-to-all-start.4) | async-done | bytes 1966112 | tf_op jit(solution)/shard_map/all_to_all | solution.py:57
  316.1 3.1 fusion.63
  319.1 1.2 multiply_reduce_fusion.1
  320.8 1.1 copy-done.3
  323.1 0.9 copy-done.7
  323.9 7.8 %fusion.58 = bf16[12,64,512]{2,1,0:T(8,128)(2,1)} fusion(bf16[512,12,64]{0,2,1:T(8,128)(2,1)S(1)} %bitcast.138, f32[12,512,512]{1,2,0:T(8,128)} %copy-done, f32[12,512]{1,0:T(8,128)S(1)} %log_add_fusion), kind=kOutput, calls=%fused_computation.97 | convolution fusion | flops 409337856 | bytes 14180352 | tf_op jit(solution)/shard_map/while/body/eval_jaxpr/hqk,qhd->khd/dot_general | solution.py:258
  331.7 7.7 %multiply_reduce_fusion = (f32[12,512]{1,0:T(8,128)S(1)}, f32[12,512,512]{1,2,0:T(8,128)S(1)}) fusion(f32[12,512,512]{1,2,0:T(8,128)} %copy-done, f32[12,512]{1,0:T(8,128)S(1)} %log_add_fusion, bf16[512,12,64]{0,2,1:T(8,128)(2,1)} %bitcast.139, bf16[512,12,64]{0,2,1:T(8,128)(2,1)} %bitcast.150), kind=kOutput, calls=%fused_computation.18 | convolution fusion | flops 412084224 | bytes 26787840 | tf_op jit(solution)/shard_map/while/body/eval_jaxpr/qhd,khd->hqk/dot_general | solution.py:244
  339.5 5.5 %multiply_convert_fusion.1 = bf16[12,512,512]{1,2,0:T(8,128)(2,1)} fusion(f32[12,512,512]{1,2,0:T(8,128)S(1)} %get-tuple-element.185, f32[12,512,512]{1,2,0:T(8,128)S(1)} %bitcast.132, f32[12,512]{1,0:T(8,128)S(1)} %get-tuple-element.184, f32[12,512]{1,0:T(8,128)S(1)} %log_add_fusion), kind=kLoop, calls=%fused_computation.17 | loop fusion | flops 12582912 | bytes 31506432 | tf_op jit(solution)/shard_map/while/body/eval_jaxpr/convert_element_type | solution.py:248
  345.0 10.4 %fusion.77 = bf16[12,32]{1,0:T(8,128)(2,1)S(1)} fusion(s32[512,512]{0,1:T(8,128)} %copy-done.10, bf16[12,512,512]{1,2,0:T(8,128)(2,1)} %multiply_convert_fusion.1), kind=kOutput, calls=%fused_computation.111 | convolution fusion | flops 209715584 | bytes 7340800 | tf_op jit(solution)/shard_map/while/body/eval_jaxpr/hqk,qkb->hb/dot_general | solution.py:264
  355.4 5.8 %multiply_convert_fusion.3 = bf16[12,64,512]{2,1,0:T(8,128)(2,1)} fusion(bf16[512,12,64]{0,2,1:T(8,128)(2,1)S(1)} %bitcast.141, bf16[12,512,512]{1,2,0:T(8,128)(2,1)} %multiply_convert_fusion.1), kind=kOutput, calls=%fused_computation.87 | convolution fusion | flops 403439616 | bytes 7864320 | tf_op jit(solution)/shard_map/while/body/eval_jaxpr/hqk,qhd->khd/dot_general | solution.py:255
  361.3 1.1 multiply_convert_fusion.4
  362.5 6.6 %fusion.53 = (bf16[768]{0:T(1024)(128)(2,1)S(1)}, f32[512]{0:T(512)}, f32[512,768]{1,0:T(8,128)}) fusion(bf16[512,768]{1,0:T(8,128)(2,1)S(1)} %copy-done.14, f32[512]{0:T(512)S(1)} %copy-done.26, f32[768]{0:T(1024)S(1)} %copy-done.22, bf16[768,2304]{1,0:T(8,128)(2,1)} %constant_dynamic-update-slice_fusion, bf16[512,768]{0,1:T(8,128)(2,1)} %bitcast.161, ...), kind=kOutput, calls=%fused_computation.82 | convolution fusion | flops 1821768448 | bytes 8266240 | tf_op jit(solution)/shard_map/dot_general | solution.py:36
  369.4 2.3 fusion.57
  371.7 2.9 convolution_convert_fusion.1
  375.9 1.8 fusion.39
  377.6 1.1 copy-done.2
  378.7 5.2 %collective-permute-done = bf16[1664,768]{1,0:T(8,128)(2,1)} collective-permute-done((bf16[1664,768]{1,0:T(8,128)(2,1)}, bf16[1664,768]{1,0:T(8,128)(2,1)}, u32[]{:S(2)}, u32[]{:S(2)}) %collective-permute-start) | collective-permute-done | bytes 2555936 | tf_op jit(solution)/shard_map/ppermute | solution.py:313
  383.9 3.1 fusion.19
  387.0 34.4 %all_to_all.39 = bf16[4,416,768]{2,1,0:T(8,128)(2,1)} all-to-all(bf16[4,416,768]{2,1,0:T(8,128)(2,1)S(1)} %bitcast.137), channel_id=1, replica_groups=mesh['dp'=4,'expert'=4,'wshard'=2] {'dp'}, dimensions={0} | all-to-all | bytes 5111808 | tf_op jit(solution)/shard_map/all_to_all | solution.py:316
  421.4 3.1 reduce_sum.186
  424.5 19.4 %all_to_all.40 = bf16[4,104,768]{2,1,0:T(8,128)(2,1)S(1)} all-to-all(bf16[4,104,768]{2,1,0:T(8,128)(2,1)} %bitcast.153), channel_id=1, replica_groups=mesh['dp'=4,'expert'=4,'wshard'=2] {'expert'}, dimensions={0} | all-to-all | bytes 1277952 | tf_op jit(solution)/shard_map/all_to_all | solution.py:316
  444.1 17.4 %all_gather.38 = bf16[416,768]{1,0:T(8,128)(2,1)} all-gather(bf16[104,768]{1,0:T(8,128)(2,1)S(1)} %reduce_sum.187), channel_id=1, replica_groups=mesh['dp'=4,'expert'=4,'wshard'=2] {'expert'}, dimensions={0}, use_global_device_ids=true | all-gather | bytes 798720 | tf_op jit(solution)/shard_map/all_gather | solution.py:321
  461.5 3.0 fusion.52
  464.5 2.9 convert_element_type.378
  467.4 2.8 convert_element_type.377
  470.3 27.5 %all-gather.17.cloned.1.call-done = bf16[1664,768]{1,0:T(8,128)(2,1)} async-done(((bf16[416,768]{1,0:T(8,128)(2,1)}), bf16[1664,768]{1,0:T(8,128)(2,1)}) %all-gather.17.cloned.1.call-update) | async-done | bytes 2555920 | tf_op jit(solution)/shard_map/all_gather | solution.py:321
  497.8 0.9 slice_convert_fusion.1
  499.5 1.0 fusion.122
  502.6 2.3 fusion.120
  (166 shorter events, 15.9 us)
Async XLA Ops:
  7.2 6.6 %copy-start.20 = (s32[512,2]{0,1:T(2,128)S(1)}, s32[512,2]{0,1:T(2,128)}, u32[]{:S(2)}) copy-start(s32[512,2]{0,1:T(2,128)} %param.17) | copy-start | bytes 12292
  7.2 6.6 %copy-start.17 = (bf16[512,768]{1,0:T(8,128)(2,1)S(1)}, bf16[512,768]{1,0:T(8,128)(2,1)}, u32[]{:S(2)}) copy-start(bf16[512,768]{1,0:T(8,128)(2,1)} %param.15) | copy-start | bytes 2359300
  7.2 33.5 %all-gather.9.cloned.1.call-start = ((), (), s32[]{:S(2)}) async-start(), calls=%async_computation.9 | async-start | bytes 1769472 | tf_op jit(solution)/shard_map/all_gather | solution.py:100
  7.9 35.3 %all-gather.11.cloned.1.call-start = ((), (), s32[]{:S(2)}) async-start(), calls=%async_computation.10 | async-start | bytes 1769472 | tf_op jit(solution)/shard_map/all_gather | solution.py:101
  8.7 37.0 %all-gather.13.cloned.1.call-start = ((), (), s32[]{:S(2)}) async-start(), calls=%async_computation.11 | async-start | bytes 1769472 | tf_op jit(solution)/shard_map/all_gather | solution.py:102
  16.4 7.7 %copy-start.31 = (bf16[384]{0:T(512)(128)(2,1)S(1)}, bf16[384]{0:T(512)(128)(2,1)}, u32[]{:S(2)}) copy-start(bf16[384]{0:T(512)(128)(2,1)} %param.18) | copy-start | bytes 2308
  16.4 9.7 %copy-start.32 = (bf16[384]{0:T(512)(128)(2,1)S(1)}, bf16[384]{0:T(512)(128)(2,1)}, u32[]{:S(2)}) copy-start(bf16[384]{0:T(512)(128)(2,1)} %param.19) | copy-start | bytes 2308
  16.4 11.6 %copy-start.12 = (bf16[512,768]{1,0:T(8,128)(2,1)S(1)}, bf16[512,768]{1,0:T(8,128)(2,1)}, u32[]{:S(2)}) copy-start(bf16[512,768]{1,0:T(8,128)(2,1)} %param.14) | copy-start | bytes 2359300
  16.4 11.8 %copy-start.29 = (bf16[6,32]{1,0:T(8,128)(2,1)S(1)}, bf16[6,32]{1,0:T(8,128)(2,1)}, u32[]{:S(2)}) copy-start(bf16[6,32]{1,0:T(8,128)(2,1)} %param.25) | copy-start | bytes 1156
  16.4 13.6 %copy-start.28 = (bf16[384,8]{0,1:T(8,128)(2,1)S(1)}, bf16[384,8]{0,1:T(8,128)(2,1)}, u32[]{:S(2)}) copy-start(bf16[384,8]{0,1:T(8,128)(2,1)} %param.24) | copy-start | bytes 18436
  16.4 15.6 %copy-start.24 = (s32[1,512]{1,0:T(1,128)S(1)}, s32[1,512]{1,0:T(1,128)}, u32[]{:S(2)}) copy-start(s32[1,512]{1,0:T(1,128)} %param.16) | copy-start | bytes 6148
  16.4 65.1 %all-to-all-start = ((bf16[8,160,768]{2,1,0:T(8,128)(2,1)}), bf16[8,160,768]{2,1,0:T(8,128)(2,1)}, u32[]{:S(2)}, u32[]{:S(2)}) async-start(bf16[8,160,768]{2,1,0:T(8,128)(2,1)} %bitcast.154), calls=%async_computation | async-start | bytes 3932160 | tf_op jit(solution)/shard_map/all_to_all | solution.py:52
  22.9 54.3 %all-gather.15.cloned.1.call-start = ((), (), s32[]{:S(2)}) async-start(), calls=%async_computation.12 | async-start | bytes 1769472 | tf_op jit(solution)/shard_map/all_gather | solution.py:103
  24.1 16.6 %copy-start.10 = (s32[512,512]{0,1:T(8,128)}, s32[512,512]{0,1:T(8,128)S(1)}, u32[]{:S(2)}) copy-start(s32[512,512]{0,1:T(8,128)S(1)} %convert_add_fusion.3) | copy-start | bytes 3145732
  26.1 22.0 %copy-start.21 = (f32[768]{0:T(1024)}, f32[768]{0:T(1024)S(1)}, u32[]{:S(2)}) copy-start(f32[768]{0:T(1024)S(1)} %reshape.430) | copy-start | bytes 9220
  28.2 19.9 %copy-start.25 = (f32[512]{0:T(512)}, f32[512]{0:T(512)S(1)}, u32[]{:S(2)}) copy-start(f32[512]{0:T(512)S(1)} %add_rsqrt_fusion.1) | copy-start | bytes 6148
  52.7 16.6 %copy-start.5 = (bf16[512,768]{0,1:T(8,128)(2,1)}, bf16[512,768]{0,1:T(8,128)(2,1)S(1)}, u32[]{:S(2)}) copy-start(bf16[512,768]{0,1:T(8,128)(2,1)S(1)} %copy.123) | copy-start | bytes 2359300
  53.0 16.3 %copy-start.8 = (bf16[512,768]{0,1:T(8,128)(2,1)}, bf16[512,768]{0,1:T(8,128)(2,1)S(1)}, u32[]{:S(2)}) copy-start(bf16[512,768]{0,1:T(8,128)(2,1)S(1)} %copy.122) | copy-start | bytes 2359300
  53.3 17.9 %copy-start.11 = (bf16[512,768]{0,1:T(8,128)(2,1)}, bf16[512,768]{0,1:T(8,128)(2,1)S(1)}, u32[]{:S(2)}) copy-start(bf16[512,768]{0,1:T(8,128)(2,1)S(1)} %copy.121) | copy-start | bytes 2359300
  69.3 4.7 copy-start
  74.0 3.2 copy-start.13
  81.6 10.5 %all-to-all-start.2 = ((f32[8,1,160]{2,1,0:T(1,128)}), f32[8,1,160]{2,1,0:T(1,128)S(1)}, u32[]{:S(2)}, u32[]{:S(2)}) async-start(f32[8,1,160]{2,1,0:T(1,128)} %all_to_all.26), calls=%async_computation.2 | async-start | bytes 16384 | tf_op jit(solution)/shard_map/all_to_all | solution.py:42
  92.1 50.6 %all-to-all-start.1 = ((bf16[8,160,768]{2,1,0:T(8,128)(2,1)}), bf16[8,160,768]{2,1,0:T(8,128)(2,1)}, u32[]{:S(2)}, u32[]{:S(2)}) async-start(bf16[8,160,768]{2,1,0:T(8,128)(2,1)} %bitcast.157), calls=%async_computation.1 | async-start | bytes 3932160 | tf_op jit(solution)/shard_map/all_to_all | solution.py:42
  96.5 368.1 %reduce-scatter.5.cloned.1.call-start = ((), (), s32[]{:S(2)}) async-start(), calls=%async_computation.15 | async-start | bytes 5898240 | tf_op jit(solution)/shard_map/reduce_scatter | solution.py:203
  151.5 5.5 %copy-start.34 = (f32[1280,3072]{1,0:T(8,128)}, f32[1280,3072]{1,0:T(8,128)S(1)}, u32[]{:S(2)}) copy-start(f32[1280,3072]{1,0:T(8,128)S(1)} %fusion.25) | copy-start | bytes 47185924
  156.9 27.1 %slice-start.3 = ((s8[4718592]{0:T(1024)(128)(4,1)}), s8[4194304]{0:T(1024)(128)(4,1)S(1)}, s32[]{:S(2)}) async-start(s8[4718592]{0:T(1024)(128)(4,1)} %bitcast.186), calls=%async_computation.19 | async-start | bytes 8388608
  169.6 14.4 %slice-start.4 = ((s8[4718592]{0:T(1024)(128)(4,1)}), s8[524288]{0:T(1024)(128)(4,1)S(1)}, s32[]{:S(2)}) async-start(s8[4718592]{0:T(1024)(128)(4,1)} %bitcast.186), calls=%async_computation.20 | async-start | bytes 1048576
  214.8 50.6 %all-to-all-start.3 = ((bf16[8,160,768]{2,1,0:T(8,128)(2,1)}), bf16[8,160,768]{2,1,0:T(8,128)(2,1)}, u32[]{:S(2)}, u32[]{:S(2)}) async-start(bf16[8,160,768]{2,1,0:T(8,128)(2,1)} %bitcast.156), calls=%async_computation.3 | async-start | bytes 3932160 | tf_op jit(solution)/shard_map/all_to_all | solution.py:47
  265.4 50.6 %all-to-all-start.4 = ((bf16[8,160,768]{2,1,0:T(8,128)(2,1)}), bf16[8,160,768]{2,1,0:T(8,128)(2,1)}, u32[]{:S(2)}, u32[]{:S(2)}) async-start(bf16[8,160,768]{2,1,0:T(8,128)(2,1)} %bitcast.155), calls=%async_computation.4 | async-start | bytes 3932160 | tf_op jit(solution)/shard_map/all_to_all | solution.py:57
  269.8 197.6 %reduce-scatter.3.cloned.1.call-start = ((), (), s32[]{:S(2)}) async-start(), calls=%async_computation.14 | async-start | bytes 5898240 | tf_op jit(solution)/shard_map/reduce_scatter | solution.py:206
  270.4 3.1 copy-start.18
  270.4 227.4 %all-gather.17.cloned.1.call-start = ((), (), s32[]{:S(2)}) async-start(), calls=%async_computation.13 | async-start | bytes 3194880 | tf_op jit(solution)/shard_map/all_gather | solution.py:321
  320.3 1.6 copy-start.33
  320.8 1.1 copy-start.3
  323.1 0.9 copy-start.7
  323.9 15.5 %slice-start = ((s8[12582912]{0:T(1024)(128)(4,1)}), s8[4194304]{0:T(1024)(128)(4,1)S(1)}, s32[]{:S(2)}) async-start(s8[12582912]{0:T(1024)(128)(4,1)} %bitcast.131), calls=%async_computation.16 | async-start | bytes 8388608
  323.9 15.5 %slice-start.1 = ((s8[12582912]{0:T(1024)(128)(4,1)}), s8[4194304]{0:T(1024)(128)(4,1)S(1)}, s32[]{:S(2)}) async-start(s8[12582912]{0:T(1024)(128)(4,1)} %bitcast.131), calls=%async_computation.17 | async-start | bytes 8388608
  331.7 7.8 %slice-start.2 = ((s8[12582912]{0:T(1024)(128)(4,1)}), s8[4194304]{0:T(1024)(128)(4,1)S(1)}, s32[]{:S(2)}) async-start(s8[12582912]{0:T(1024)(128)(4,1)} %bitcast.131), calls=%async_computation.18 | async-start | bytes 8388608
  345.0 10.4 %copy-start.9 = (bf16[512,768]{0,1:T(8,128)(2,1)S(1)}, bf16[512,768]{0,1:T(8,128)(2,1)}, u32[]{:S(2)}) copy-start(bf16[512,768]{0,1:T(8,128)(2,1)} %copy-done.8) | copy-start | bytes 2359300
  355.4 5.8 %copy-start.1 = (bf16[12,512,512]{1,2,0:T(8,128)(2,1)S(1)}, bf16[12,512,512]{1,2,0:T(8,128)(2,1)}, u32[]{:S(2)}) copy-start(bf16[12,512,512]{1,2,0:T(8,128)(2,1)} %multiply_convert_fusion.1) | copy-start | bytes 18874372
  355.4 5.8 %copy-start.6 = (bf16[512,768]{0,1:T(8,128)(2,1)S(1)}, bf16[512,768]{0,1:T(8,128)(2,1)}, u32[]{:S(2)}) copy-start(bf16[512,768]{0,1:T(8,128)(2,1)} %copy-done.5) | copy-start | bytes 2359300
  361.2 1.2 copy-start.23
  361.2 1.3 copy-start.14
  361.2 1.3 copy-start.22
  361.2 1.3 copy-start.26
  362.5 6.9 %copy-start.4 = (f32[512,768]{1,0:T(8,128)S(1)}, f32[512,768]{1,0:T(8,128)}, u32[]{:S(2)}) copy-start(f32[512,768]{1,0:T(8,128)} %copy-done.3) | copy-start | bytes 4718596
  369.1 2.5 copy-start.16
  369.1 2.5 copy-start.19
  375.8 2.9 copy-start.2
  378.7 5.2 %collective-permute-start = (bf16[1664,768]{1,0:T(8,128)(2,1)}, bf16[1664,768]{1,0:T(8,128)(2,1)}, u32[]{:S(2)}, u32[]{:S(2)}) collective-permute-start(bf16[1664,768]{1,0:T(8,128)(2,1)} %fusion.39), channel_id=1, source_target_pairs={{0,1},{1,0},{2,3},{3,2},{4,5},{5,4},{6,7},{7,6},{8,9},{9,8},{10,11... | collective-permute-start | bytes 7667720 | tf_op jit(solution)/shard_map/ppermute | solution.py:313
  421.4 40.1 %copy-start.30 = (f32[512]{0:T(512)S(1)}, f32[512]{0:T(512)}, u32[]{:S(2)}) copy-start(f32[512]{0:T(512)} %get-tuple-element.157) | copy-start | bytes 6148
  421.4 40.1 %copy-start.27 = (f32[512]{0:T(512)S(1)}, f32[512]{0:T(512)}, u32[]{:S(2)}) copy-start(f32[512]{0:T(512)} %copy-done.25) | copy-start | bytes 6148
  497.8 4.4 copy-start.15
Sparse Core Ops, SparseCore 0:
  9.6 11.9 all-gather.8
  23.1 10.3 all-gather.10
  35.1 10.3 all-gather.12
  46.9 10.3 all-gather.14
  214.9 55.9 reduce-scatter.4
  273.8 57.9 reduce-scatter.2
  461.6 36.1 all-gather.16
where the time goes:
time: 522 us; the launch traced here: 512 us
  matrix products  175 us (34%)
  waiting for transfers between devices  157 us (30%)
  blocking collectives  78.8 us (15%)
  other arithmetic  32.9 us (6%)
  local copies, waits for them, and re-layouts  28.2 us (5%)
  starting transfers between devices  24.9 us (5%)
  between operations  15.1 us (3%)
    dot_general x10, matrix products, contract(): lax.dot_general(left, right, (((left_dim,), (right_dim,)), ((), ())), pre...  70.9 us
    all_to_all x2, blocking collectives, per_device(): lax.all_to_all(part.reshape(lax.axis_size(axis), -1, width), axis, split_...  53.9 us
    all_to_all x2, waiting for transfers between devices, send_rows(): lax.all_to_all(rows, ('expert', 'wshard'), split_axis=0, concat_axis=0, t...  49.1 us
    all_to_all x1, waiting for transfers between devices, send_row_grads(): lax.all_to_all(rows, ('expert', 'wshard'), split_axis=0, concat_axis=0, t...  37.9 us
    all_to_all x1, waiting for transfers between devices, send_results(): lax.all_to_all(rows, ('expert', 'wshard'), split_axis=0, concat_axis=0, t...  34.5 us
    all_gather x1, waiting for transfers between devices, per_device(): part = lax.all_gather(part, axis, axis=0, tiled=True)  27.5 us
    unnamed x88, local copies, waits for them, and re-layouts  18.2 us
    all_gather x1, blocking collectives, per_device(): part = lax.all_gather(part, axis, axis=0, tiled=True)  17.4 us
  transfers between devices with their start and end apart: 13, of which 6 were waited for; matrix products, arithmetic and copies ran while one was open for 29% of the time, Pallas kernels for 0%

commit v1 on v0

--- a/solution.py
+++ b/solution.py
@@ -179,8 +179,8 @@
         + jnp.where(takes_second, gates[:, 1][None, :], 0.0),
         axis=1,
     )
+    arrived, gate_slots = lax.optimization_barrier((arrived, gate_slots))
     gate_arrived = send_rows(gate_slots.reshape(experts, capacity)).reshape(-1)
-    arrived, gate_arrived = lax.optimization_barrier((arrived, gate_arrived))
     rows_in = arrived.reshape(-1, width)
     pre = jnp.dot(rows_in, expert_in[0], preferred_element_type=jnp.float32)
     hidden = jax.nn.gelu(pre).astype(jnp.bfloat16)
@@ -192,21 +192,22 @@
     grad_arrived = (gate_arrived[:, None] * cotangent_arrived.astype(jnp.float32)).astype(
         jnp.bfloat16
     )
-    grad_out_weight = contract(hidden, grad_arrived, 0, 0).astype(jnp.bfloat16)
     grad_hidden = contract(grad_arrived, expert_out[0], 1, 1)
     unused, gelu_back = jax.vjp(jax.nn.gelu, pre)
     grad_pre = gelu_back(grad_hidden)[0].astype(jnp.bfloat16)
+    returned, grad_pre = lax.optimization_barrier((returned, grad_pre))
+    grad_rows = contract(grad_pre, expert_in[0], 1, 1).astype(jnp.bfloat16)
+    grad_rows, grad_pre, hidden = lax.optimization_barrier((grad_rows, grad_pre, hidden))
+    grad_out_weight = contract(hidden, grad_arrived, 0, 0).astype(jnp.bfloat16)
     grad_in_weight = contract(rows_in, grad_pre, 0, 0).astype(jnp.bfloat16)
-    grad_pre, grad_in_weight, grad_out_weight = lax.optimization_barrier(
-        (grad_pre, grad_in_weight, grad_out_weight)
-    )
     expert_out_sum = lax.psum_scatter(
         grad_out_weight[None], "dp", scatter_dimension=1, tiled=True
     )
     expert_in_sum = lax.psum_scatter(grad_in_weight[None], "dp", scatter_dimension=2, tiled=True)
-    grad_rows = contract(grad_pre, expert_in[0], 1, 1).astype(jnp.bfloat16)
-    returned, grad_rows = lax.optimization_barrier((returned, grad_rows))
     grad_back = send_row_grads(grad_rows.reshape(experts, capacity, width)).reshape(-1, width)
+    grad_back, unused_out, unused_in = lax.optimization_barrier(
+        (grad_back, grad_out_weight, grad_in_weight)
+    )
     picked_first = jnp.dot(pick_first, returned, preferred_element_type=jnp.float32)
     picked_second = jnp.dot(pick_second, returned, preferred_element_type=jnp.float32)
     mixed = resid + (gates[:, :1] * picked_first + gates[:, 1:] * picked_second)

time: 522 us -> 494 us (0.946); the launches traced: 512 us -> 489 us
  waiting for transfers between devices: 157 us -> 132 us
    all_to_all x1, waiting for transfers between devices: 37.9 us -> 26.7 us  [send_row_grads(): lax.all_to_all(rows, ('expert', 'wshard'), split_axis=0, concat_axis=0, t...]
    all_to_all x1, waiting for transfers between devices: 34.5 us -> 25.1 us  [send_results(): lax.all_to_all(rows, ('expert', 'wshard'), split_axis=0, concat_axis=0, t...]
    all_to_all x2, waiting for transfers between devices: 49.1 us -> 43.3 us  [send_rows(): lax.all_to_all(rows, ('expert', 'wshard'), split_axis=0, concat_axis=0, t...]
    dot_general x1, matrix products: 8.74 us -> 14.3 us  [per_device(): pre = jnp.dot(rows_in, expert_in[0], preferred_element_type=jnp.float32)]
  transfers between devices with their start and end apart: 13 -> 13, of which waited for: 6 -> 6; matrix products, arithmetic and copies ran while one was open for 29% -> 41% of each run, Pallas kernels for 0% -> 0%
where the time goes in v1:
time: 494 us; the launch traced here: 489 us
  matrix products  176 us (36%)
  waiting for transfers between devices  132 us (27%)
  blocking collectives  79.1 us (16%)
  other arithmetic  37.5 us (8%)
  starting transfers between devices  24.8 us (5%)
  local copies, waits for them, and re-layouts  24.7 us (5%)
  between operations  15.2 us (3%)
    dot_general x10, matrix products, contract(): lax.dot_general(left, right, (((left_dim,), (right_dim,)), ((), ())), pre...  67.4 us
    all_to_all x2, blocking collectives, per_device(): lax.all_to_all(part.reshape(lax.axis_size(axis), -1, width), axis, split_...  53.9 us
    all_to_all x2, waiting for transfers between devices, send_rows(): lax.all_to_all(rows, ('expert', 'wshard'), split_axis=0, concat_axis=0, t...  43.3 us
    all_gather x1, waiting for transfers between devices, per_device(): part = lax.all_gather(part, axis, axis=0, tiled=True)  27.5 us
    all_to_all x1, waiting for transfers between devices, send_row_grads(): lax.all_to_all(rows, ('expert', 'wshard'), split_axis=0, concat_axis=0, t...  26.7 us
    all_to_all x1, waiting for transfers between devices, send_results(): lax.all_to_all(rows, ('expert', 'wshard'), split_axis=0, concat_axis=0, t...  25.1 us
    dot_general x1, matrix products, block_scores(): jnp.einsum('qhd,khd->hqk', query_block, key_rows, preferred_element_type=...  18 us
    all_gather x1, blocking collectives, per_device(): part = lax.all_gather(part, axis, axis=0, tiled=True)  17.4 us
  transfers between devices with their start and end apart: 13, of which 6 were waited for; matrix products, arithmetic and copies ran while one was open for 41% of the time, Pallas kernels for 0%

profile of v1, /device:TPU:0, one launch (start us, length us, event | category | flops | bytes accessed | tf_op | source)
XLA Modules:
  0.0 489.2 jit_solution(4221825895379649462)
XLA Ops:
  9.4 0.8 copy.126
  10.4 2.3 reduce-window.6
  13.8 2.6 convolution_convert_fusion.5
  16.4 6.5 %all-to-all-start = ((bf16[8,160,768]{2,1,0:T(8,128)(2,1)}), bf16[8,160,768]{2,1,0:T(8,128)(2,1)}, u32[]{:S(2)}, u32[]{:S(2)}) async-start(bf16[8,160,768]{2,1,0:T(8,128)(2,1)} %bitcast.158), calls=%async_computation | async-start | bytes 3932160 | tf_op jit(solution)/shard_map/all_to_all | solution.py:52
  24.1 2.0 all-gather
  26.1 1.8 all-gather.2
  28.2 2.0 all-gather.1
  30.5 8.5 %fusion.1 = f32[512,512,12]{0,2,1:T(8,128)} fusion(bf16[12,32,1]{1,0,2:T(8,128)(2,1)S(1)} %reshape.432, s32[512,512]{0,1:T(8,128)S(1)} %convert_add_fusion.3), kind=kOutput, calls=%fused_computation.2 | convolution fusion | flops 209715200 | bytes 13632256 | tf_op jit(solution)/shard_map/while/body/eval_jaxpr/qkb,hb->hqk/dot_general | solution.py:68
  39.0 2.4 constant_dynamic-update-slice_fusion.2
  41.4 2.5 constant_dynamic-update-slice_fusion.1
  43.9 1.6 all-gather.13.cloned.1.call-done
  45.5 2.5 constant_dynamic-update-slice_fusion
  48.0 4.1 convolution_convert_fusion.3
  52.9 18.0 %fusion.127 = (f32[12,512]{1,0:T(8,128)S(1)}, f32[12,512,512]{1,2,0:T(8,128)}) fusion(f32[512,512,12]{0,2,1:T(8,128)} %fusion.1, bf16[512,12,64]{0,2,1:T(8,128)(2,1)S(1)} %bitcast.144, bf16[512,12,64]{0,2,1:T(8,128)(2,1)S(1)} %bitcast.139, pred[512,512]{0,1:T(8,128)(4,1)S(1)} %fusion.97), kind=kOutput, calls=%fused_computation.188 | convolution fusion | flops 415229952 | bytes 27025408 | tf_op jit(solution)/shard_map/while/body/eval_jaxpr/qhd,khd->hqk/dot_general | solution.py:69
  71.2 6.8 %fusion.12 = f32[12,512]{1,0:T(8,128)S(1)} fusion(f32[12,512,512]{1,2,0:T(8,128)} %get-tuple-element.182, f32[12,512]{1,0:T(8,128)S(1)} %get-tuple-element.181), kind=kLoop, calls=%fused_computation.22 | loop fusion | flops 6285312 | bytes 12632064 | tf_op jit(solution)/shard_map/while/body/eval_jaxpr/reduce_sum | solution.py:154
  78.0 1.6 copy-done
  79.6 2.5 fusion.61
  82.2 2.4 multiply_reduce_fusion.3
  84.8 2.6 convolution_convert_fusion.4
  87.5 5.0 %all-to-all-start.1 = ((bf16[8,160,768]{2,1,0:T(8,128)(2,1)}), bf16[8,160,768]{2,1,0:T(8,128)(2,1)}, u32[]{:S(2)}, u32[]{:S(2)}) async-start(bf16[8,160,768]{2,1,0:T(8,128)(2,1)} %bitcast.161), calls=%async_computation.1 | async-start | bytes 3932160 | tf_op jit(solution)/shard_map/all_to_all | solution.py:42
  92.5 2.0 all_gather.37
  95.5 43.3 %all-to-all-done.1 = bf16[8,160,768]{2,1,0:T(8,128)(2,1)} async-done(((bf16[8,160,768]{2,1,0:T(8,128)(2,1)}), bf16[8,160,768]{2,1,0:T(8,128)(2,1)}, u32[]{:S(2)}, u32[]{:S(2)}) %all-to-all-start.1) | async-done | bytes 1966112 | tf_op jit(solution)/shard_map/all_to_all | solution.py:42
  139.5 3.3 all-to-all-start.2
  142.8 14.3 %multiply_convert_fusion = (bf16[1280,3072]{1,0:T(8,128)(2,1)S(1)}, f32[1280,3072]{1,0:T(8,128)}) fusion(bf16[1280,768]{1,0:T(8,128)(2,1)} %bitcast.16, bf16[1,768,3072]{2,1,0:T(8,128)(2,1)} %param.26), kind=kOutput, calls=%fused_computation.14 | convolution fusion | flops 6075187200 | bytes 30277632 | tf_op jit(solution)/shard_map/dot_general | solution.py:185
  157.2 3.1 copy-done.35
  160.3 9.7 %fusion.30 = bf16[1280,768]{1,0:T(8,128)(2,1)} fusion(bf16[1280,3072]{1,0:T(8,128)(2,1)S(1)} %get-tuple-element.93, bf16[1,3072,768]{2,1,0:T(8,128)(2,1)} %param.27), kind=kOutput, calls=%fused_computation.48 | convolution fusion | flops 6040780800 | bytes 14548992 | tf_op jit(solution)/shard_map/dot_general | solution.py:187
  170.1 5.0 %all-to-all-start.3 = ((bf16[8,160,768]{2,1,0:T(8,128)(2,1)}), bf16[8,160,768]{2,1,0:T(8,128)(2,1)}, u32[]{:S(2)}, u32[]{:S(2)}) async-start(bf16[8,160,768]{2,1,0:T(8,128)(2,1)} %bitcast.160), calls=%async_computation.3 | async-start | bytes 3932160 | tf_op jit(solution)/shard_map/all_to_all | solution.py:47
  175.1 21.3 %fusion.10 = bf16[1280,3072]{1,0:T(8,128)(2,1)} fusion(f32[1280,3072]{1,0:T(8,128)} %get-tuple-element.186, bf16[1,3072,768]{2,1,0:T(8,128)(2,1)} %param.27, bf16[1280,768]{1,0:T(8,128)(2,1)} %bitcast.13, f32[1280]{0:T(1024)S(1)} %reshape.403), kind=kOutput, calls=%fused_computation.13 | convolution fusion | flops 6121390080 | bytes 30282752 | tf_op jit(solution)/shard_map/dot_general | solution.py:36
  196.4 25.1 %all-to-all-done.3 = bf16[8,160,768]{2,1,0:T(8,128)(2,1)} async-done(((bf16[8,160,768]{2,1,0:T(8,128)(2,1)}), bf16[8,160,768]{2,1,0:T(8,128)(2,1)}, u32[]{:S(2)}, u32[]{:S(2)}) %all-to-all-start.3) | async-done | bytes 1966112 | tf_op jit(solution)/shard_map/all_to_all | solution.py:47
  221.4 11.1 %fusion.27 = bf16[1280,768]{1,0:T(8,128)(2,1)} fusion(bf16[1280,3072]{1,0:T(8,128)(2,1)} %fusion.10, bf16[1,768,3072]{2,1,0:T(8,128)(2,1)} %param.26), kind=kOutput, calls=%fused_computation.47 | convolution fusion | flops 6040780800 | bytes 14548992 | tf_op jit(solution)/shard_map/dot_general | solution.py:36
  232.6 10.2 %convolution_convert_fusion = bf16[3072,768]{1,0:T(8,128)(2,1)} fusion(bf16[1280,3072]{1,0:T(8,128)(2,1)S(1)} %copy-done.36, bf16[1280,768]{1,0:T(8,128)(2,1)} %bitcast.13, f32[1280]{0:T(1024)S(1)} %reshape.403), kind=kOutput, calls=%fused_computation.32 | convolution fusion | flops 6045106176 | bytes 14554112 | tf_op jit(solution)/shard_map/dot_general | solution.py:36
  242.8 4.3 all-to-all-start.4
  247.6 3.5 fusion.34
  251.1 4.0 fusion.55
  255.8 10.8 %convolution_convert_fusion.2 = bf16[768,3072]{1,0:T(8,128)(2,1)} fusion(bf16[1280,768]{1,0:T(8,128)(2,1)} %bitcast.16, bf16[1280,3072]{1,0:T(8,128)(2,1)} %fusion.10), kind=kOutput, calls=%fused_computation.34 | convolution fusion | flops 6042157056 | bytes 14548992 | tf_op jit(solution)/shard_map/dot_general | solution.py:36
  266.7 26.7 %all-to-all-done.4 = bf16[8,160,768]{2,1,0:T(8,128)(2,1)} async-done(((bf16[8,160,768]{2,1,0:T(8,128)(2,1)}), bf16[8,160,768]{2,1,0:T(8,128)(2,1)}, u32[]{:S(2)}, u32[]{:S(2)}) %all-to-all-start.4) | async-done | bytes 1966112 | tf_op jit(solution)/shard_map/all_to_all | solution.py:57
  293.4 3.0 fusion.63
  296.4 1.2 multiply_reduce_fusion.1
  298.1 1.1 copy-done.3
  300.4 0.9 copy-done.7
  301.3 7.7 %fusion.58 = bf16[12,64,512]{2,1,0:T(8,128)(2,1)} fusion(bf16[512,12,64]{0,2,1:T(8,128)(2,1)S(1)} %bitcast.142, f32[12,512,512]{1,2,0:T(8,128)} %get-tuple-element.182, f32[12,512]{1,0:T(8,128)S(1)} %log_add_fusion), kind=kOutput, calls=%fused_computation.97 | convolution fusion | flops 409337856 | bytes 14180352 | tf_op jit(solution)/shard_map/while/body/eval_jaxpr/hqk,qhd->khd/dot_general | solution.py:259
  308.9 7.7 %multiply_reduce_fusion = (f32[12,512]{1,0:T(8,128)S(1)}, f32[12,512,512]{1,2,0:T(8,128)S(1)}) fusion(f32[12,512,512]{1,2,0:T(8,128)} %get-tuple-element.182, f32[12,512]{1,0:T(8,128)S(1)} %log_add_fusion, bf16[512,12,64]{0,2,1:T(8,128)(2,1)} %bitcast.143, bf16[512,12,64]{0,2,1:T(8,128)(2,1)} %bitcast.154), kind=kOutput, calls=%fused_computation.18 | convolution fusion | flops 412084224 | bytes 26787840 | tf_op jit(solution)/shard_map/while/body/eval_jaxpr/qhd,khd->hqk/dot_general | solution.py:245
  316.7 5.3 %multiply_convert_fusion.1 = bf16[12,512,512]{1,2,0:T(8,128)(2,1)} fusion(f32[12,512,512]{1,2,0:T(8,128)S(1)} %get-tuple-element.189, f32[12,512,512]{1,2,0:T(8,128)S(1)} %bitcast.136, f32[12,512]{1,0:T(8,128)S(1)} %get-tuple-element.188, f32[12,512]{1,0:T(8,128)S(1)} %log_add_fusion), kind=kLoop, calls=%fused_computation.17 | loop fusion | flops 12582912 | bytes 31506432 | tf_op jit(solution)/shard_map/while/body/eval_jaxpr/convert_element_type | solution.py:249
  322.0 10.5 %fusion.77 = bf16[12,32]{1,0:T(8,128)(2,1)S(1)} fusion(s32[512,512]{0,1:T(8,128)} %copy-done.10, bf16[12,512,512]{1,2,0:T(8,128)(2,1)} %multiply_convert_fusion.1), kind=kOutput, calls=%fused_computation.111 | convolution fusion | flops 209715584 | bytes 7340800 | tf_op jit(solution)/shard_map/while/body/eval_jaxpr/hqk,qkb->hb/dot_general | solution.py:265
  332.5 5.9 %multiply_convert_fusion.3 = bf16[12,64,512]{2,1,0:T(8,128)(2,1)} fusion(bf16[512,12,64]{0,2,1:T(8,128)(2,1)S(1)} %bitcast.145, bf16[12,512,512]{1,2,0:T(8,128)(2,1)} %multiply_convert_fusion.1), kind=kOutput, calls=%fused_computation.87 | convolution fusion | flops 403439616 | bytes 7864320 | tf_op jit(solution)/shard_map/while/body/eval_jaxpr/hqk,qhd->khd/dot_general | solution.py:256
  338.5 1.1 multiply_convert_fusion.4
  339.7 6.6 %fusion.53 = (bf16[768]{0:T(1024)(128)(2,1)S(1)}, f32[512]{0:T(512)}, f32[512,768]{1,0:T(8,128)}) fusion(bf16[512,768]{1,0:T(8,128)(2,1)S(1)} %copy-done.14, f32[512]{0:T(512)S(1)} %copy-done.27, f32[768]{0:T(1024)S(1)} %copy-done.23, bf16[768,2304]{1,0:T(8,128)(2,1)} %constant_dynamic-update-slice_fusion, bf16[512,768]{0,1:T(8,128)(2,1)} %bitcast.165, ...), kind=kOutput, calls=%fused_computation.82 | convolution fusion | flops 1821768448 | bytes 8266240 | tf_op jit(solution)/shard_map/dot_general | solution.py:36
  346.6 2.3 fusion.57
  348.9 2.9 convolution_convert_fusion.1
  353.1 1.7 fusion.39
  354.8 1.2 copy-done.2
  356.0 5.2 %collective-permute-done = bf16[1664,768]{1,0:T(8,128)(2,1)} collective-permute-done((bf16[1664,768]{1,0:T(8,128)(2,1)}, bf16[1664,768]{1,0:T(8,128)(2,1)}, u32[]{:S(2)}, u32[]{:S(2)}) %collective-permute-start) | collective-permute-done | bytes 2555936 | tf_op jit(solution)/shard_map/ppermute | solution.py:314
  361.2 3.1 fusion.19
  364.2 34.5 %all_to_all.39 = bf16[4,416,768]{2,1,0:T(8,128)(2,1)} all-to-all(bf16[4,416,768]{2,1,0:T(8,128)(2,1)S(1)} %bitcast.141), channel_id=1, replica_groups=mesh['dp'=4,'expert'=4,'wshard'=2] {'dp'}, dimensions={0} | all-to-all | bytes 5111808 | tf_op jit(solution)/shard_map/all_to_all | solution.py:317
  398.7 3.1 reduce_sum.186
  401.8 19.4 %all_to_all.40 = bf16[4,104,768]{2,1,0:T(8,128)(2,1)S(1)} all-to-all(bf16[4,104,768]{2,1,0:T(8,128)(2,1)} %bitcast.157), channel_id=1, replica_groups=mesh['dp'=4,'expert'=4,'wshard'=2] {'expert'}, dimensions={0} | all-to-all | bytes 1277952 | tf_op jit(solution)/shard_map/all_to_all | solution.py:317
  421.4 17.4 %all_gather.38 = bf16[416,768]{1,0:T(8,128)(2,1)} all-gather(bf16[104,768]{1,0:T(8,128)(2,1)S(1)} %reduce_sum.187), channel_id=1, replica_groups=mesh['dp'=4,'expert'=4,'wshard'=2] {'expert'}, dimensions={0}, use_global_device_ids=true | all-gather | bytes 798720 | tf_op jit(solution)/shard_map/all_gather | solution.py:322
  438.8 3.0 fusion.52
  441.8 2.9 convert_element_type.378
  444.7 2.8 convert_element_type.377
  447.6 27.5 %all-gather.17.cloned.1.call-done = bf16[1664,768]{1,0:T(8,128)(2,1)} async-done(((bf16[416,768]{1,0:T(8,128)(2,1)}), bf16[1664,768]{1,0:T(8,128)(2,1)}) %all-gather.17.cloned.1.call-update) | async-done | bytes 2555920 | tf_op jit(solution)/shard_map/all_gather | solution.py:322
  475.1 0.9 slice_convert_fusion.1
  476.8 1.0 fusion.122
  479.9 2.3 fusion.120
  (165 shorter events, 15.7 us)
Async XLA Ops:
  7.2 6.6 %copy-start.21 = (s32[512,2]{0,1:T(2,128)S(1)}, s32[512,2]{0,1:T(2,128)}, u32[]{:S(2)}) copy-start(s32[512,2]{0,1:T(2,128)} %param.17) | copy-start | bytes 12292
  7.2 6.6 %copy-start.18 = (bf16[512,768]{1,0:T(8,128)(2,1)S(1)}, bf16[512,768]{1,0:T(8,128)(2,1)}, u32[]{:S(2)}) copy-start(bf16[512,768]{1,0:T(8,128)(2,1)} %param.15) | copy-start | bytes 2359300
  7.2 31.8 %all-gather.9.cloned.1.call-start = ((), (), s32[]{:S(2)}) async-start(), calls=%async_computation.9 | async-start | bytes 1769472 | tf_op jit(solution)/shard_map/all_gather | solution.py:100
  7.9 33.4 %all-gather.11.cloned.1.call-start = ((), (), s32[]{:S(2)}) async-start(), calls=%async_computation.10 | async-start | bytes 1769472 | tf_op jit(solution)/shard_map/all_gather | solution.py:101
  8.7 36.8 %all-gather.13.cloned.1.call-start = ((), (), s32[]{:S(2)}) async-start(), calls=%async_computation.11 | async-start | bytes 1769472 | tf_op jit(solution)/shard_map/all_gather | solution.py:102
  16.4 7.7 %copy-start.32 = (bf16[384]{0:T(512)(128)(2,1)S(1)}, bf16[384]{0:T(512)(128)(2,1)}, u32[]{:S(2)}) copy-start(bf16[384]{0:T(512)(128)(2,1)} %param.18) | copy-start | bytes 2308
  16.4 9.7 %copy-start.33 = (bf16[384]{0:T(512)(128)(2,1)S(1)}, bf16[384]{0:T(512)(128)(2,1)}, u32[]{:S(2)}) copy-start(bf16[384]{0:T(512)(128)(2,1)} %param.19) | copy-start | bytes 2308
  16.4 11.5 %copy-start.12 = (bf16[512,768]{1,0:T(8,128)(2,1)S(1)}, bf16[512,768]{1,0:T(8,128)(2,1)}, u32[]{:S(2)}) copy-start(bf16[512,768]{1,0:T(8,128)(2,1)} %param.14) | copy-start | bytes 2359300
  16.4 11.8 %copy-start.30 = (bf16[6,32]{1,0:T(8,128)(2,1)S(1)}, bf16[6,32]{1,0:T(8,128)(2,1)}, u32[]{:S(2)}) copy-start(bf16[6,32]{1,0:T(8,128)(2,1)} %param.25) | copy-start | bytes 1156
  16.4 13.8 %copy-start.25 = (s32[1,512]{1,0:T(1,128)S(1)}, s32[1,512]{1,0:T(1,128)}, u32[]{:S(2)}) copy-start(s32[1,512]{1,0:T(1,128)} %param.16) | copy-start | bytes 6148
  16.4 68.4 %all-to-all-start = ((bf16[8,160,768]{2,1,0:T(8,128)(2,1)}), bf16[8,160,768]{2,1,0:T(8,128)(2,1)}, u32[]{:S(2)}, u32[]{:S(2)}) async-start(bf16[8,160,768]{2,1,0:T(8,128)(2,1)} %bitcast.158), calls=%async_computation | async-start | bytes 3932160 | tf_op jit(solution)/shard_map/all_to_all | solution.py:52
  22.9 59.2 %all-gather.15.cloned.1.call-start = ((), (), s32[]{:S(2)}) async-start(), calls=%async_computation.12 | async-start | bytes 1769472 | tf_op jit(solution)/shard_map/all_gather | solution.py:103
  24.1 14.9 %copy-start.10 = (s32[512,512]{0,1:T(8,128)}, s32[512,512]{0,1:T(8,128)S(1)}, u32[]{:S(2)}) copy-start(s32[512,512]{0,1:T(8,128)S(1)} %convert_add_fusion.3) | copy-start | bytes 3145732
  26.1 21.9 %copy-start.22 = (f32[768]{0:T(1024)}, f32[768]{0:T(1024)S(1)}, u32[]{:S(2)}) copy-start(f32[768]{0:T(1024)S(1)} %reshape.430) | copy-start | bytes 9220
  28.2 19.8 %copy-start.26 = (f32[512]{0:T(512)}, f32[512]{0:T(512)S(1)}, u32[]{:S(2)}) copy-start(f32[512]{0:T(512)S(1)} %add_rsqrt_fusion.1) | copy-start | bytes 6148
  52.5 18.3 %copy-start.5 = (bf16[512,768]{0,1:T(8,128)(2,1)}, bf16[512,768]{0,1:T(8,128)(2,1)S(1)}, u32[]{:S(2)}) copy-start(bf16[512,768]{0,1:T(8,128)(2,1)S(1)} %copy.123) | copy-start | bytes 2359300
  52.8 18.0 %copy-start.8 = (bf16[512,768]{0,1:T(8,128)(2,1)}, bf16[512,768]{0,1:T(8,128)(2,1)S(1)}, u32[]{:S(2)}) copy-start(bf16[512,768]{0,1:T(8,128)(2,1)S(1)} %copy.122) | copy-start | bytes 2359300
  71.1 6.8 %copy-start.11 = (bf16[512,768]{0,1:T(8,128)(2,1)}, bf16[512,768]{0,1:T(8,128)(2,1)S(1)}, u32[]{:S(2)}) copy-start(bf16[512,768]{0,1:T(8,128)(2,1)S(1)} %copy.121) | copy-start | bytes 2359300
  71.2 8.4 %copy-start = (f32[12,512,512]{1,2,0:T(8,128)S(1)}, f32[12,512,512]{1,2,0:T(8,128)}, u32[]{:S(2)}) copy-start(f32[12,512,512]{1,2,0:T(8,128)} %get-tuple-element.182) | copy-start | bytes 37748740
  79.6 2.5 copy-start.13
  82.1 2.7 copy-start.16
  87.5 5.0 %copy-start.29 = (bf16[384,8]{0,1:T(8,128)(2,1)S(1)}, bf16[384,8]{0,1:T(8,128)(2,1)}, u32[]{:S(2)}) copy-start(bf16[384,8]{0,1:T(8,128)(2,1)} %param.24) | copy-start | bytes 18436
  87.5 51.4 %all-to-all-start.1 = ((bf16[8,160,768]{2,1,0:T(8,128)(2,1)}), bf16[8,160,768]{2,1,0:T(8,128)(2,1)}, u32[]{:S(2)}, u32[]{:S(2)}) async-start(bf16[8,160,768]{2,1,0:T(8,128)(2,1)} %bitcast.161), calls=%async_computation.1 | async-start | bytes 3932160 | tf_op jit(solution)/shard_map/all_to_all | solution.py:42
  139.5 30.5 %all-to-all-start.2 = ((f32[8,1,160]{2,1,0:T(1,128)}), f32[8,1,160]{2,1,0:T(1,128)S(1)}, u32[]{:S(2)}, u32[]{:S(2)}) async-start(f32[8,1,160]{2,1,0:T(1,128)} %all_to_all.26), calls=%async_computation.2 | async-start | bytes 16384 | tf_op jit(solution)/shard_map/all_to_all | solution.py:42
  157.2 3.1 copy-start.35
  170.1 51.4 %all-to-all-start.3 = ((bf16[8,160,768]{2,1,0:T(8,128)(2,1)}), bf16[8,160,768]{2,1,0:T(8,128)(2,1)}, u32[]{:S(2)}, u32[]{:S(2)}) async-start(bf16[8,160,768]{2,1,0:T(8,128)(2,1)} %bitcast.160), calls=%async_computation.3 | async-start | bytes 3932160 | tf_op jit(solution)/shard_map/all_to_all | solution.py:47
  175.1 266.7 %reduce-scatter.5.cloned.1.call-start = ((), (), s32[]{:S(2)}) async-start(), calls=%async_computation.15 | async-start | bytes 5898240 | tf_op jit(solution)/shard_map/reduce_scatter | solution.py:203
  221.4 11.1 %copy-start.36 = (bf16[1280,3072]{1,0:T(8,128)(2,1)S(1)}, bf16[1280,3072]{1,0:T(8,128)(2,1)}, u32[]{:S(2)}) copy-start(bf16[1280,3072]{1,0:T(8,128)(2,1)} %copy-done.35) | copy-start | bytes 23592964
  242.8 50.6 %all-to-all-start.4 = ((bf16[8,160,768]{2,1,0:T(8,128)(2,1)}), bf16[8,160,768]{2,1,0:T(8,128)(2,1)}, u32[]{:S(2)}, u32[]{:S(2)}) async-start(bf16[8,160,768]{2,1,0:T(8,128)(2,1)} %bitcast.159), calls=%async_computation.4 | async-start | bytes 3932160 | tf_op jit(solution)/shard_map/all_to_all | solution.py:57
  247.1 197.6 %reduce-scatter.3.cloned.1.call-start = ((), (), s32[]{:S(2)}) async-start(), calls=%async_computation.14 | async-start | bytes 5898240 | tf_op jit(solution)/shard_map/reduce_scatter | solution.py:206
  247.6 3.5 copy-start.19
  266.7 208.4 %all-gather.17.cloned.1.call-start = ((), (), s32[]{:S(2)}) async-start(), calls=%async_computation.13 | async-start | bytes 3194880 | tf_op jit(solution)/shard_map/all_gather | solution.py:322
  297.6 1.6 copy-start.34
  298.1 1.1 copy-start.3
  300.4 0.9 copy-start.7
  301.3 15.4 %slice-start = ((s8[12582912]{0:T(1024)(128)(4,1)}), s8[4194304]{0:T(1024)(128)(4,1)S(1)}, s32[]{:S(2)}) async-start(s8[12582912]{0:T(1024)(128)(4,1)} %bitcast.135), calls=%async_computation.16 | async-start | bytes 8388608
  301.3 15.4 %slice-start.1 = ((s8[12582912]{0:T(1024)(128)(4,1)}), s8[4194304]{0:T(1024)(128)(4,1)S(1)}, s32[]{:S(2)}) async-start(s8[12582912]{0:T(1024)(128)(4,1)} %bitcast.135), calls=%async_computation.17 | async-start | bytes 8388608
  308.9 7.8 %slice-start.2 = ((s8[12582912]{0:T(1024)(128)(4,1)}), s8[4194304]{0:T(1024)(128)(4,1)S(1)}, s32[]{:S(2)}) async-start(s8[12582912]{0:T(1024)(128)(4,1)} %bitcast.135), calls=%async_computation.18 | async-start | bytes 8388608
  322.0 10.5 %copy-start.9 = (bf16[512,768]{0,1:T(8,128)(2,1)S(1)}, bf16[512,768]{0,1:T(8,128)(2,1)}, u32[]{:S(2)}) copy-start(bf16[512,768]{0,1:T(8,128)(2,1)} %copy-done.8) | copy-start | bytes 2359300
  332.5 6.0 %copy-start.1 = (bf16[12,512,512]{1,2,0:T(8,128)(2,1)S(1)}, bf16[12,512,512]{1,2,0:T(8,128)(2,1)}, u32[]{:S(2)}) copy-start(bf16[12,512,512]{1,2,0:T(8,128)(2,1)} %multiply_convert_fusion.1) | copy-start | bytes 18874372
  332.5 5.9 %copy-start.6 = (bf16[512,768]{0,1:T(8,128)(2,1)S(1)}, bf16[512,768]{0,1:T(8,128)(2,1)}, u32[]{:S(2)}) copy-start(bf16[512,768]{0,1:T(8,128)(2,1)} %copy-done.5) | copy-start | bytes 2359300
  338.4 1.2 copy-start.24
  338.4 1.3 copy-start.14
  338.4 1.3 copy-start.23
  338.4 1.3 copy-start.27
  339.7 6.9 %copy-start.4 = (f32[512,768]{1,0:T(8,128)S(1)}, f32[512,768]{1,0:T(8,128)}, u32[]{:S(2)}) copy-start(f32[512,768]{1,0:T(8,128)} %copy-done.3) | copy-start | bytes 4718596
  346.3 2.6 copy-start.17
  346.3 2.6 copy-start.20
  353.1 2.9 copy-start.2
  356.0 5.2 %collective-permute-start = (bf16[1664,768]{1,0:T(8,128)(2,1)}, bf16[1664,768]{1,0:T(8,128)(2,1)}, u32[]{:S(2)}, u32[]{:S(2)}) collective-permute-start(bf16[1664,768]{1,0:T(8,128)(2,1)} %fusion.39), channel_id=1, source_target_pairs={{0,1},{1,0},{2,3},{3,2},{4,5},{5,4},{6,7},{7,6},{8,9},{9,8},{10,11... | collective-permute-start | bytes 7667720 | tf_op jit(solution)/shard_map/ppermute | solution.py:314
  398.7 40.1 %copy-start.31 = (f32[512]{0:T(512)S(1)}, f32[512]{0:T(512)}, u32[]{:S(2)}) copy-start(f32[512]{0:T(512)} %get-tuple-element.159) | copy-start | bytes 6148
  398.7 40.1 %copy-start.28 = (f32[512]{0:T(512)S(1)}, f32[512]{0:T(512)}, u32[]{:S(2)}) copy-start(f32[512]{0:T(512)} %copy-done.26) | copy-start | bytes 6148
  475.1 4.4 copy-start.15
Sparse Core Ops, SparseCore 0:
  9.6 11.9 all-gather.8
  23.1 10.3 all-gather.10
  35.1 10.3 all-gather.12
  46.9 10.3 all-gather.14
  242.9 55.9 reduce-scatter.4
  301.7 57.0 reduce-scatter.2
  438.9 36.1 all-gather.16
